TPU v7x, 32 devices: a whole 2x2x4 slice. The times are simulated.
32 devices in a mesh: groups: 2 (over y), blk: 4 (over z), help: 4 (over x, core).
Axes of the slice: x: 2, y: 2, z: 4, core: 2. Of those that a mesh axis runs over, the one named last changes fastest.
Arguments:
- users: float32 [16384, 128], P(('groups', 'blk', 'help')), parts along dimension 0, may hold values from -2.5 to 2.5
- items: float32 [16384, 128], P(('groups', 'blk', 'help')), parts along dimension 0, may hold values from -2.5 to 2.5
- user_state: float32 [16384], P(('groups', 'blk', 'help')), parts along dimension 0, may hold values from 5 to 50
- item_state: float32 [16384], P(('groups', 'blk', 'help')), parts along dimension 0, may hold values from 5 to 50
- ratings: bfloat16 [8, 4, 2, 16, 128, 128], P(('groups', 'blk'), 'help'), parts along dimension 0
- masks: bfloat16 [8, 4, 2, 16, 128, 128], P(('groups', 'blk'), 'help'), parts along dimension 0, may hold values from 0 to 2, as said below
- tile_cells: int32 [8, 4, 2, 16], P(('groups', 'blk'), 'help'), parts along dimension 0, may hold values from 0 to 15, as said below
- tile_count: int32 [8, 4, 2], P(('groups', 'blk'), 'help'), parts along dimension 0, may hold values from 1 to 16, as said below
Outputs:
- users_out: float32 [16384, 128], P(('groups', 'blk', 'help')), parts along dimension 0
- items_out: float32 [16384, 128], P(('groups', 'blk', 'help')), parts along dimension 0
- user_state_out: float32 [16384], P(('groups', 'blk', 'help')), parts along dimension 0
- item_state_out: float32 [16384], P(('groups', 'blk', 'help')), parts along dimension 0
- loss: float32 [2], P('groups'), parts along dimension 0
There are 2 independent parts, one for each index of `groups`. A program takes and returns all parts, laid end to end along the dimension named above; each array names one. Nothing has to cross between parts.
Inputs may be any that keep to these rules, and one draw needn't show every extreme that they name: `tile_cells`: slots are in any order; each user tile and item tile pair of a stratum appears in exactly one slot. `tile_count`: some position of each draw has all 16 slots live. `masks`: entries of slots at or past the live count are zero; unrated entries are zero.
All inputs are finite; a program needn't handle non-finite values.
Results may differ from a plain program's by a relative error of at most 0.0016.
Values may be sent and summed in bfloat16 or wider, within the bound.
A program may use at most 64 MiB of HBM per device.

v0:
```python
import math

import jax
import jax.numpy as jnp
from jax import lax
from jax.sharding import PartitionSpec as P

INNER = 2


EPS = 1e-06
LEARN = 0.03
DECAY = 0.02


def passed_along(block, axis, distance):
    devices = range(lax.axis_size(axis))
    route = [((i - distance) % len(devices), i) for i in devices]
    return lax.ppermute(block, axis, route)


def tile_terms(users_narrow, items_narrow, ratings, masks, cells, live, item_tiles, width):
    tile = ratings.shape[-1]
    rank = users_narrow.shape[-1]
    user_tiles = users_narrow.shape[0] // tile
    user_grid = users_narrow.reshape(user_tiles, tile, rank)
    item_grid = items_narrow.reshape(item_tiles, tile, rank)
    blocks = (jnp.maximum(live, 0) + width - 1) // width

    def one_block(index, carry):
        grad_users, grad_items, squared, counted = carry
        start = index * width
        values = lax.dynamic_slice_in_dim(ratings, start, width, 0)
        weights_raw = lax.dynamic_slice_in_dim(masks, start, width, 0)
        picked = lax.dynamic_slice_in_dim(cells, start, width, 0)
        slots = start + jnp.arange(width, dtype=jnp.int32)
        weight = weights_raw.astype(jnp.float32) * (slots < live).astype(jnp.float32)[:, None, None]
        user_ids = picked // item_tiles
        item_ids = picked % item_tiles
        user_part = jnp.take(user_grid, user_ids, axis=0)
        item_part = jnp.take(item_grid, item_ids, axis=0)
        predicted = jnp.einsum(
            "tar,tbr->tab", user_part, item_part, preferred_element_type=jnp.float32
        )
        error = weight * (predicted - values.astype(jnp.float32))
        error_narrow = error.astype(jnp.bfloat16)
        user_terms = jnp.einsum(
            "tab,tbr->tar", error_narrow, item_part, preferred_element_type=jnp.float32
        )
        item_terms = jnp.einsum(
            "tab,tar->tbr", error_narrow, user_part, preferred_element_type=jnp.float32
        )
        user_onehot = (
            user_ids[:, None] == jnp.arange(user_tiles, dtype=jnp.int32)[None, :]
        ).astype(jnp.float32)
        item_onehot = (
            item_ids[:, None] == jnp.arange(item_tiles, dtype=jnp.int32)[None, :]
        ).astype(jnp.float32)
        grad_users = grad_users + jnp.einsum(
            "tk,tar->kar", user_onehot, user_terms, precision=lax.Precision.HIGHEST
        )
        grad_items = grad_items + jnp.einsum(
            "tk,tbr->kbr", item_onehot, item_terms, precision=lax.Precision.HIGHEST
        )
        return (grad_users, grad_items, squared + jnp.sum(error * error), counted + jnp.sum(weight))

    start_carry = (
        jnp.zeros((user_tiles, tile, rank), jnp.float32),
        jnp.zeros((item_tiles, tile, rank), jnp.float32),
        jnp.float32(0.0),
        jnp.float32(0.0),
    )
    return lax.fori_loop(0, blocks, one_block, start_carry)


def adagrad(factors, state, grads):
    state_new = state + jnp.mean(grads * grads, axis=-1)
    return (factors - LEARN * grads / jnp.sqrt(state_new + EPS)[:, None], state_new)


def on_device(users, items, user_state, item_state, ratings, masks, tile_cells, tile_count):
    ratings = ratings[0, 0]
    masks = masks[0, 0]
    tile_cells = tile_cells[0, 0]
    tile_count = tile_count[0, 0]
    strata = ratings.shape[0]
    capacity = ratings.shape[1]
    tile = ratings.shape[-1]
    item_tiles = items.shape[0] // tile
    halfway = capacity // 2
    width = math.gcd(4, halfway)
    squared = jnp.float32(0.0)
    counted = jnp.float32(0.0)
    for stratum in range(strata):
        values = ratings[stratum]
        weights_all = masks[stratum]
        picked = tile_cells[stratum]
        live = tile_count[stratum]
        for inner in range(INNER):
            users_narrow = users.astype(jnp.bfloat16)
            items_narrow = items.astype(jnp.bfloat16)
            grad_users, grad_items, part_sq, part_count = tile_terms(
                users_narrow, items_narrow, values, weights_all, picked, live, item_tiles, width
            )
            squared = squared + part_sq
            counted = counted + part_count
            grad_users = grad_users.reshape(users.shape) + DECAY * users
            grad_items = grad_items.reshape(items.shape) + DECAY * items
            users, user_state = adagrad(users, user_state, grad_users)
            items, item_state = adagrad(items, item_state, grad_items)
        items, item_state = passed_along((items, item_state), "blk", 1)
    totals = lax.psum((squared, counted), ("blk", "help"))
    loss = (totals[0] / totals[1]).reshape(1)
    return (users, items, user_state, item_state, loss)


def solution(mesh):
    in_specs = (
        P(("groups", "blk", "help"), None),
        P(("groups", "blk", "help"), None),
        P(("groups", "blk", "help")),
        P(("groups", "blk", "help")),
        P(("groups", "blk"), "help", None, None, None, None),
        P(("groups", "blk"), "help", None, None, None, None),
        P(("groups", "blk"), "help", None, None),
        P(("groups", "blk"), "help", None),
    )
    out_specs = (
        P(("groups", "blk", "help"), None),
        P(("groups", "blk", "help"), None),
        P(("groups", "blk", "help")),
        P(("groups", "blk", "help")),
        P("groups"),
    )
    return jax.shard_map(
        on_device, mesh=mesh, in_specs=in_specs, out_specs=out_specs, check_vma=False
    )
```

profile of v0, /device:TPU:0, one launch (start us, length us, event | category | flops | bytes accessed | tf_op | source)
XLA Modules:
  0.0 182.0 jit_solution(1196137146540283936)
XLA Ops:
  0.6 1.3 fusion.73
  2.7 0.8 slice_bitcast_fusion.4
  3.4 1.0 convert_element_type.144
  4.5 1.7 slice_bitcast_fusion
  6.3 8.0 %while.72 = (s32[]{:T(128)}, f32[4,128,128]{2,0,1:T(4,128)S(1)}, f32[4,128,128]{2,0,1:T(4,128)S(1)}, f32[]{:T(128)}, f32[]{:T(128)}, /*index=5*/s32[]{:T(128)}, ...) while((s32[]{:T(128)}, f32[4,128,128]{2,0,1:T(4,128)S(1)}, ...), condition=%wide.region_3.5_spmd, body=%wide.region_0.4_spmd.sunk | while | flops 57739476 | bytes 3940939 | solution.py:73
  6.3 0.8 compare_and_fusion.16
  8.4 1.0 multiply_reduce_fusion.16
  9.6 1.1 convolution_add_fusion.16
  10.9 1.1 convolution_add_fusion.17
  12.7 0.8 fusion.126
  14.3 0.9 copy-done
  17.0 8.7 %while.73 = (s32[]{:T(128)}, f32[4,128,128]{2,0,1:T(4,128)S(1)}, f32[4,128,128]{2,0,1:T(4,128)S(1)}, f32[]{:T(128)}, f32[]{:T(128)}, /*index=5*/s32[]{:T(128)}, ...) while((s32[]{:T(128)}, f32[4,128,128]{2,0,1:T(4,128)S(1)}, ...), condition=%wide.region_9.11_spmd, body=%wide.region_6.10_spmd.sunk | while | flops 57739476 | bytes 8135299 | solution.py:73
  17.1 0.8 compare_and_fusion.18
  19.2 1.8 %multiply_reduce_fusion.17 = (f32[]{:T(128)}, bf16[4,128,128]{2,1,0:T(8,128)(2,1)S(1)}) fusion(bf16[16,128,128]{2,1,0:T(8,128)(2,1)} %copy-done.2, s32[]{:T(128)S(6)} %select_n.278, bf16[4,128,128]{2,1,0:T(8,128)(2,1)S(1)} %gather_fusion.2, pred[4]{0:T(512)(128)(4,1)S(1)} %get-tuple-element.1133, bf16[4,128,128]{2,1,0:T(8,128)(2,1)S(1)} %gather_fusion.3, ...), kind=kOutput, calls=%fused_computation.50.clone.1 | convolution fusion | flops 17432576 | bytes 655392 | tf_op jit(solution)/shard_map/while/body/tar,tbr->tab/dot_general | solution.py:42
  21.2 1.1 convolution_add_fusion.18
  22.6 1.1 convolution_add_fusion.19
  24.3 0.7 fusion.135
  26.1 19.7 %collective-permute-start = (f32[512,128]{1,0:T(8,128)S(1)}, f32[512,128]{1,0:T(8,128)S(1)}, u32[]{:S(2)}, u32[]{:S(2)}) collective-permute-start(f32[512,128]{1,0:T(8,128)S(1)} %divide_subtract_fusion.4), channel_id=1, source_target_pairs={{12,0},{0,4},{4,8},{8,12},{13,1},{1,5},{5,9},{9,13},{14,2},{2,6},{... | collective-permute-start | bytes 786440 | tf_op jit(solution)/shard_map/ppermute | solution.py:19
  45.8 1.6 collective-permute-start.1
  48.4 3.0 %collective-permute-done = f32[512,128]{1,0:T(8,128)S(1)} collective-permute-done((f32[512,128]{1,0:T(8,128)S(1)}, f32[512,128]{1,0:T(8,128)S(1)}, u32[]{:S(2)}, u32[]{:S(2)}) %collective-permute-start) | collective-permute-done | bytes 262176 | tf_op jit(solution)/shard_map/ppermute | solution.py:19
  51.5 15.4 %while.74 = (s32[]{:T(128)}, f32[4,128,128]{2,0,1:T(4,128)S(1)}, f32[4,128,128]{2,0,1:T(4,128)S(1)}, f32[]{:T(128)}, f32[]{:T(128)}, /*index=5*/s32[]{:T(128)}, ...) while((s32[]{:T(128)}, f32[4,128,128]{2,0,1:T(4,128)S(1)}, ...), condition=%wide.region_15.17_spmd, body=%wide.region_12.16_spmd.sunk | while | flops 57739476 | bytes 3940939 | solution.py:73
  51.5 0.7 compare_and_fusion.20
  53.6 0.9 multiply_reduce_fusion.18
  54.7 1.1 convolution_add_fusion.20
  56.1 1.1 convolution_add_fusion.21
  57.8 0.7 fusion.144
  59.2 0.7 compare_and_fusion.20
  61.3 0.9 multiply_reduce_fusion.18
  62.4 1.1 convolution_add_fusion.20
  63.8 1.1 convolution_add_fusion.21
  65.5 0.7 fusion.144
  67.7 15.4 %while.75 = (s32[]{:T(128)}, f32[4,128,128]{2,0,1:T(4,128)S(1)}, f32[4,128,128]{2,0,1:T(4,128)S(1)}, f32[]{:T(128)}, f32[]{:T(128)}, /*index=5*/s32[]{:T(128)}, ...) while((s32[]{:T(128)}, f32[4,128,128]{2,0,1:T(4,128)S(1)}, ...), condition=%wide.region_21.23_spmd, body=%wide.region_18.22_spmd.sunk | while | flops 57739476 | bytes 3940939 | solution.py:73
  67.7 0.7 compare_and_fusion.22
  69.8 0.9 multiply_reduce_fusion.19
  70.9 1.1 convolution_add_fusion.22
  72.3 1.1 convolution_add_fusion.23
  74.0 0.7 fusion.153
  75.4 0.7 compare_and_fusion.22
  77.5 0.9 multiply_reduce_fusion.19
  78.6 1.1 convolution_add_fusion.22
  80.0 1.1 convolution_add_fusion.23
  81.7 0.7 fusion.153
  83.7 0.6 add_sqrt_fusion.1
  84.3 2.8 %collective-permute-start.3 = (f32[512]{0:T(512)S(1)}, f32[512]{0:T(512)S(1)}, u32[]{:S(2)}, u32[]{:S(2)}) collective-permute-start(f32[512]{0:T(512)S(1)} %get-tuple-element.773), channel_id=1, source_target_pairs={{12,0},{0,4},{4,8},{8,12},{13,1},{1,5},{5,9},{9,13},{14,2},{2,6},{... | collective-permute-start | bytes 6152 | tf_op jit(solution)/shard_map/ppermute | solution.py:19
  87.0 0.8 divide_subtract_fusion.1
  87.9 90.4 %all-reduce = (f32[]{:T(128)}, f32[]{:T(128)}) all-reduce(f32[]{:T(128)S(6)} %add.385, f32[]{:T(128)S(6)} %add.388), channel_id=1, replica_groups=mesh['groups'=2,'blk'=4,'help'=4] {'blk','help'}, use_global_device_ids=true, to_apply=%region_24.26 | all-reduce | flops 2 | bytes 16 | tf_op jit(solution)/shard_map/psum | solution.py:112
  179.6 0.7 copy.126
  180.3 0.6 copy.127
  (109 shorter events, 14.5 us)
Async XLA Ops:
  0.6 3.8 %copy-start.1 = (f32[512,128]{1,0:T(8,128)S(1)}, f32[512,128]{1,0:T(8,128)}, u32[]{:S(2)}) copy-start(f32[512,128]{1,0:T(8,128)} %param.19) | copy-start | bytes 786436
  14.3 1.0 copy-start
  15.2 0.7 copy-start.5
  16.1 0.7 copy-start.4
  17.1 0.8 copy-start.2
  22.6 3.1 %copy-start.3 = (bf16[16,128,128]{2,1,0:T(8,128)(2,1)S(1)}, bf16[16,128,128]{2,1,0:T(8,128)(2,1)}, u32[]{:S(2)}) copy-start(bf16[16,128,128]{2,1,0:T(8,128)(2,1)} %copy-done.2) | copy-start | bytes 1572868 | tf_op jit(solution)/shard_map/while
  26.1 25.3 %collective-permute-start = (f32[512,128]{1,0:T(8,128)S(1)}, f32[512,128]{1,0:T(8,128)S(1)}, u32[]{:S(2)}, u32[]{:S(2)}) collective-permute-start(f32[512,128]{1,0:T(8,128)S(1)} %divide_subtract_fusion.4), channel_id=1, source_target_pairs={{12,0},{0,4},{4,8},{8,12},{13,1},{1,5},{5,9},{9,13},{14,2},{2,6},{... | collective-permute-start | bytes 786440 | tf_op jit(solution)/shard_map/ppermute | solution.py:19
  45.8 21.6 %collective-permute-start.1 = (f32[512]{0:T(512)S(1)}, f32[512]{0:T(512)S(1)}, u32[]{:S(2)}, u32[]{:S(2)}) collective-permute-start(f32[512]{0:T(512)S(1)} %get-tuple-element.781), channel_id=1, source_target_pairs={{12,0},{0,4},{4,8},{8,12},{13,1},{1,5},{5,9},{9,13},{14,2},{2,6},{... | collective-permute-start | bytes 6152 | tf_op jit(solution)/shard_map/ppermute | solution.py:19
  83.5 96.1 %collective-permute-start.2 = (f32[512,128]{1,0:T(8,128)S(1)}, f32[512,128]{1,0:T(8,128)S(1)}, u32[]{:S(2)}, u32[]{:S(2)}) collective-permute-start(f32[512,128]{1,0:T(8,128)S(1)} %divide_subtract_fusion), channel_id=1, source_target_pairs={{12,0},{0,4},{4,8},{8,12},{13,1},{1,5},{5,9},{9,13},{14,2},{2,6},{... | collective-permute-start | bytes 786440 | tf_op jit(solution)/shard_map/ppermute | solution.py:19
  84.3 95.3 %collective-permute-start.3 = (f32[512]{0:T(512)S(1)}, f32[512]{0:T(512)S(1)}, u32[]{:S(2)}, u32[]{:S(2)}) collective-permute-start(f32[512]{0:T(512)S(1)} %get-tuple-element.773), channel_id=1, source_target_pairs={{12,0},{0,4},{4,8},{8,12},{13,1},{1,5},{5,9},{9,13},{14,2},{2,6},{... | collective-permute-start | bytes 6152 | tf_op jit(solution)/shard_map/ppermute | solution.py:19
where the time goes:
time: 185 us; the launch traced here: 182 us
  blocking collectives  90.4 us (49%)
  starting transfers between devices  24.1 us (13%)
  matrix products  22.4 us (12%)
  local copies, waits for them, and re-layouts  14.4 us (8%)
  other arithmetic  14.4 us (8%)
  loops' own time  8.5 us (5%)
  between operations  4.84 us (3%)
  waiting for transfers between devices  2.99 us (2%)
    psum x1, blocking collectives, on_device(): totals = lax.psum((squared, counted), ('blk', 'help'))  90.4 us
    ppermute x4, starting transfers between devices, passed_along(): return lax.ppermute(block, axis, route)  24.1 us
    another operation x4, loops' own time, tile_terms(): return lax.fori_loop(0, blocks, one_block, start_carry)  8.5 us
    dot_general x6, matrix products, one_block(): jnp.einsum('tk,tbr->kbr', item_onehot, item_terms, precision=lax.Precisio...  6.48 us
    dot_general x6, matrix products, one_block(): jnp.einsum('tk,tar->kar', user_onehot, user_terms, precision=lax.Precisio...  6.48 us
    dot_general x6, matrix products, one_block(): jnp.einsum('tar,tbr->tab', user_part, item_part, preferred_element_type=j...  6.46 us
    reduce_sum x6, other arithmetic, one_block(): jnp.sum(weight)  4.53 us
    and x6, other arithmetic, one_block(): item_part = jnp.take(item_grid, item_ids, axis=0)  4.49 us
  transfers between devices with their start and end apart: 4, of which 1 were waited for; matrix products, arithmetic and copies ran while one was open for 8% of the time, Pallas kernels for 0%

commit v1 on v0

v1 whole, which is shorter than its diff:
```python
import functools

import jax
import jax.numpy as jnp
from jax import lax
from jax.experimental import pallas as pl
from jax.experimental.pallas import tpu as pltpu
from jax.sharding import PartitionSpec as P

INNER = 2
EPS = 1e-06
LEARN = 0.03
DECAY = 0.02
LEVELS = 32767.0
CHUNK = 256
MESH = pl.DeviceIdType.MESH
F32 = jnp.float32
BF16 = jnp.bfloat16


def inverse_cells(cells_ref, stratum, capacity):
    picked = [cells_ref[0, 0, stratum, slot] for slot in range(capacity)]
    where = []
    for cell in range(capacity):
        found = jnp.int32(0)
        for slot in range(1, capacity):
            found = jnp.where(picked[slot] == cell, jnp.int32(slot), found)
        where.append(found)
    return where


def encode(values):
    top = jnp.max(jnp.abs(values), axis=0, keepdims=True)
    scale = jnp.maximum(top, 1e-30) * (1.0 / LEVELS)
    codes = jnp.round(values * (1.0 / scale)).astype(jnp.int32).astype(jnp.int16)
    return codes, scale


def kernel(
    sizes,
    cells_ref, users_ref, items_ref, ustate_ref, istate_ref, ratings_ref, masks_ref,
    users_out, items_out, ustate_out, istate_out, loss_ref,
    users, items_nat, items, ustate_in, ustate_row, ustate, istate, error,
    items_back, codes_out, aux_out, codes_in, aux_in, sums_help, sums_blk,
    load_sem, store_sem, code_send, code_recv, aux_send, aux_recv,
    help_send, help_recv, blk_send, blk_recv, *tiles,
):
    strata, capacity, tile, rank, user_tiles, item_tiles, n_blk, n_help = sizes
    rat, msk = tiles[:strata], tiles[strata:]
    n_items = item_tiles * tile
    chunks = n_items // CHUNK
    per_chunk = CHUNK // tile
    my_blk = lax.axis_index("blk")
    my_help = lax.axis_index("help")
    right = lax.rem(my_blk + 1, n_blk)

    loads = {}
    plan = [("users", users_ref, users), ("items", items_ref, items_nat),
            ("ustate", ustate_ref, ustate_in), ("istate", istate_ref, istate)]
    for s in range(strata):
        plan.append((("m", s), masks_ref.at[0, 0, s], msk[s]))
        plan.append((("r", s), ratings_ref.at[0, 0, s], rat[s]))
    for number, (name, src, dst) in enumerate(plan):
        loads[name] = pltpu.make_async_copy(src, dst, load_sem.at[number])
        loads[name].start()

    barrier = pltpu.get_barrier_semaphore()
    for d in range(1, n_blk):
        pl.semaphore_signal(barrier, inc=1, device_id={"blk": lax.rem(my_blk + d, n_blk)}, device_id_type=MESH)
    for d in range(1, n_help):
        pl.semaphore_signal(barrier, inc=1, device_id={"help": lax.rem(my_help + d, n_help)}, device_id_type=MESH)

    slots = [inverse_cells(cells_ref, s, capacity) for s in range(strata)]

    loads["items"].wait()
    for i in range(item_tiles):
        items[:, i * tile:(i + 1) * tile] = items_nat[i * tile:(i + 1) * tile, :].T
    loads["istate"].wait()
    loads["ustate"].wait()
    for u in range(user_tiles):
        ustate[u * tile:(u + 1) * tile, :] = jnp.broadcast_to(ustate_in[u:u + 1, :], (tile, tile)).T
    loads["users"].wait()

    squared = jnp.zeros((8, tile), F32)
    counted = jnp.zeros((8, tile), F32)

    def shift(hop, c):
        cols = pl.ds(c * CHUNK, CHUNK)
        code = pltpu.make_async_remote_copy(
            src_ref=codes_out.at[hop, c], dst_ref=codes_in.at[hop, c],
            send_sem=code_send.at[hop, c], recv_sem=code_recv.at[hop, c],
            device_id={"blk": right}, device_id_type=MESH)
        aux = pltpu.make_async_remote_copy(
            src_ref=aux_out.at[hop, c], dst_ref=aux_in.at[hop, c],
            send_sem=aux_send.at[hop, c], recv_sem=aux_recv.at[hop, c],
            device_id={"blk": right}, device_id_type=MESH)
        return code, aux

    def fold(x):
        return x.reshape(-1, 8, tile).sum(axis=0)

    for s in range(strata):
        loads[("m", s)].wait()
        loads[("r", s)].wait()
        for inner in range(INNER):
            last = inner == INNER - 1
            un = [users[u * tile:(u + 1) * tile, :].astype(BF16) for u in range(user_tiles)]
            ut = jnp.concatenate([x.T for x in un], axis=1)
            for c in range(chunks):
                lo, hi = c * CHUNK, (c + 1) * CHUNK
                if s > 0 and inner == 0:
                    code, aux = shift(s - 1, c)
                    code.wait_recv()
                    aux.wait_recv()
                    block = codes_in[s - 1, c].astype(jnp.int32).astype(F32) * aux_in[s - 1, c, 0:1, :]
                    items[:, lo:hi] = block
                    istate[0:1, lo:hi] = aux_in[s - 1, c, 1:2, :]
                block = items[:, lo:hi]
                narrow = block.astype(BF16)
                for k in range(per_chunk):
                    items_back[lo + k * tile:lo + (k + 1) * tile, :] = narrow[:, k * tile:(k + 1) * tile].T
                for u in range(user_tiles):
                    predicted = jnp.dot(un[u], narrow, preferred_element_type=F32)
                    for k in range(per_chunk):
                        i = c * per_chunk + k
                        at = slots[s][u * item_tiles + i]
                        weight = msk[s][at].astype(F32)
                        err = weight * (predicted[:, k * tile:(k + 1) * tile] - rat[s][at].astype(F32))
                        squared = squared + fold(err * err)
                        if inner == 0:
                            counted = counted + fold(weight)
                        error[u * tile:(u + 1) * tile, i * tile:(i + 1) * tile] = err.astype(BF16)
                grad = jnp.dot(ut, error[:, lo:hi], preferred_element_type=F32) + DECAY * block
                state = istate[0:1, lo:hi] + jnp.sum(grad * grad, axis=0, keepdims=True) * (1.0 / rank)
                block = block - (LEARN * grad) * lax.rsqrt(state + EPS)
                if not last:
                    items[:, lo:hi] = block
                    istate[0:1, lo:hi] = state
                else:
                    codes, scale = encode(block)
                    codes_out[s, c] = codes
                    aux_out[s, c] = jnp.concatenate([scale, state] + [jnp.zeros_like(scale)] * 6, axis=0)
                    if s == 0 and c == 0:
                        pl.semaphore_wait(barrier, (n_blk - 1) + (n_help - 1))
                    for copy in shift(s, c):
                        copy.start()
            if s == strata - 1 and last:
                mine = jnp.concatenate(
                    [jnp.sum(squared, axis=0, keepdims=True),
                     jnp.sum(counted, axis=0, keepdims=True) * float(INNER),
                     jnp.zeros((6, tile), F32)], axis=0)
                sums_help[my_help] = mine
                helps = []
                for d in range(1, n_help):
                    helps.append(pltpu.make_async_remote_copy(
                        src_ref=sums_help.at[my_help], dst_ref=sums_help.at[my_help],
                        send_sem=help_send.at[d], recv_sem=help_recv.at[my_help],
                        device_id={"help": lax.rem(my_help + d, n_help)}, device_id_type=MESH))
                    helps[-1].start()
            for u in range(user_tiles):
                rows = slice(u * tile, (u + 1) * tile)
                own = users[rows, :]
                grad = jnp.dot(error[rows, :], items_back[...], preferred_element_type=F32) + DECAY * own
                state = ustate[rows, :] + jnp.sum(grad * grad, axis=1, keepdims=True) * (1.0 / rank)
                ustate[rows, :] = state
                users[rows, :] = own - (LEARN * grad) * lax.rsqrt(state + EPS)

    stores = [pltpu.make_async_copy(users, users_out, store_sem.at[0])]
    stores[-1].start()
    for u in range(user_tiles):
        ustate_row[u:u + 1, :] = ustate[u * tile:(u + 1) * tile, :].T[0:1, :]
    stores.append(pltpu.make_async_copy(ustate_row, ustate_out, store_sem.at[1]))
    stores[-1].start()

    def arrival(buf, axis, index, send, recv):
        return pltpu.make_async_remote_copy(
            src_ref=buf.at[index], dst_ref=buf.at[index], send_sem=send.at[0],
            recv_sem=recv.at[index], device_id={axis: index}, device_id_type=MESH)

    for d in range(1, n_help):
        arrival(sums_help, "help", lax.rem(my_help + d, n_help), help_send, help_recv).wait_recv()
    total = sums_help[0]
    for j in range(1, n_help):
        total = total + sums_help[j]
    sums_blk[my_blk] = total
    blks = []
    for d in range(1, n_blk):
        blks.append(pltpu.make_async_remote_copy(
            src_ref=sums_blk.at[my_blk], dst_ref=sums_blk.at[my_blk],
            send_sem=blk_send.at[d], recv_sem=blk_recv.at[my_blk],
            device_id={"blk": lax.rem(my_blk + d, n_blk)}, device_id_type=MESH))
        blks[-1].start()

    for c in range(chunks):
        lo = c * CHUNK
        code, aux = shift(strata - 1, c)
        code.wait_recv()
        aux.wait_recv()
        block = codes_in[strata - 1, c].astype(jnp.int32).astype(F32) * aux_in[strata - 1, c, 0:1, :]
        istate[0:1, lo:lo + CHUNK] = aux_in[strata - 1, c, 1:2, :]
        for k in range(per_chunk):
            items_nat[lo + k * tile:lo + (k + 1) * tile, :] = block[:, k * tile:(k + 1) * tile].T
        rows = pl.ds(lo, CHUNK)
        stores.append(pltpu.make_async_copy(items_nat.at[rows], items_out.at[rows], store_sem.at[3 + c]))
        stores[-1].start()
    stores.append(pltpu.make_async_copy(istate, istate_out, store_sem.at[2]))
    stores[-1].start()

    for d in range(1, n_blk):
        arrival(sums_blk, "blk", lax.rem(my_blk + d, n_blk), blk_send, blk_recv).wait_recv()
    total = sums_blk[0]
    for j in range(1, n_blk):
        total = total + sums_blk[j]
    loss_ref[0] = jnp.sum(total[0:1, :]) / jnp.sum(total[1:2, :])

    for copy in helps + blks:
        copy.wait_send()
    for hop in range(strata):
        for c in range(chunks):
            for copy in shift(hop, c):
                copy.wait_send()
    for copy in stores:
        copy.wait()


def on_device(users, items, user_state, item_state, ratings, masks, tile_cells, tile_count):
    strata, capacity, tile = ratings.shape[2], ratings.shape[3], ratings.shape[4]
    rank = users.shape[1]
    n_users, n_items = users.shape[0], items.shape[0]
    user_tiles, item_tiles = n_users // tile, n_items // tile
    n_blk, n_help = lax.axis_size("blk"), lax.axis_size("help")
    chunks = n_items // CHUNK
    sizes = (strata, capacity, tile, rank, user_tiles, item_tiles, n_blk, n_help)
    hbm = pl.BlockSpec(memory_space=pl.ANY)
    smem = pl.BlockSpec(memory_space=pltpu.SMEM)
    dma = pltpu.SemaphoreType.DMA
    outs = pl.pallas_call(
        functools.partial(kernel, sizes),
        out_shape=(
            jax.ShapeDtypeStruct(users.shape, F32),
            jax.ShapeDtypeStruct(items.shape, F32),
            jax.ShapeDtypeStruct((user_tiles, tile), F32),
            jax.ShapeDtypeStruct((1, n_items), F32),
            jax.ShapeDtypeStruct((1,), F32),
        ),
        in_specs=[smem] + [hbm] * 6,
        out_specs=(hbm, hbm, hbm, hbm, smem),
        scratch_shapes=[
            pltpu.VMEM((n_users, rank), F32),
            pltpu.VMEM((n_items, rank), F32),
            pltpu.VMEM((rank, n_items), F32),
            pltpu.VMEM((user_tiles, tile), F32),
            pltpu.VMEM((user_tiles, tile), F32),
            pltpu.VMEM((n_users, tile), F32),
            pltpu.VMEM((1, n_items), F32),
            pltpu.VMEM((n_users, n_items), BF16),
            pltpu.VMEM((n_items, rank), BF16),
            pltpu.VMEM((strata, chunks, rank, CHUNK), jnp.int16),
            pltpu.VMEM((strata, chunks, 8, CHUNK), F32),
            pltpu.VMEM((strata, chunks, rank, CHUNK), jnp.int16),
            pltpu.VMEM((strata, chunks, 8, CHUNK), F32),
            pltpu.VMEM((n_help, 8, tile), F32),
            pltpu.VMEM((n_blk, 8, tile), F32),
            dma((4 + 2 * strata,)),
            dma((3 + chunks,)),
            dma((strata, chunks)), dma((strata, chunks)),
            dma((strata, chunks)), dma((strata, chunks)),
            dma((n_help,)), dma((n_help,)),
            dma((n_blk,)), dma((n_blk,)),
        ] + [pltpu.VMEM((capacity, tile, tile), BF16)] * (2 * strata),
        compiler_params=pltpu.CompilerParams(
            collective_id=0, has_side_effects=True, vmem_limit_bytes=56 * 1024 * 1024
        ),
        name="block_steps",
    )(tile_cells, users, items, user_state.reshape(user_tiles, tile), item_state.reshape(1, n_items), ratings, masks)
    users_out, items_out, ustate_out, istate_out, loss = outs
    return users_out, items_out, ustate_out.reshape(n_users), istate_out.reshape(n_items), loss


def solution(mesh):
    in_specs = (
        P(("groups", "blk", "help"), None),
        P(("groups", "blk", "help"), None),
        P(("groups", "blk", "help")),
        P(("groups", "blk", "help")),
        P(("groups", "blk"), "help", None, None, None, None),
        P(("groups", "blk"), "help", None, None, None, None),
        P(("groups", "blk"), "help", None, None),
        P(("groups", "blk"), "help", None),
    )
    out_specs = (
        P(("groups", "blk", "help"), None),
        P(("groups", "blk", "help"), None),
        P(("groups", "blk", "help")),
        P(("groups", "blk", "help")),
        P("groups"),
    )
    return jax.shard_map(
        on_device, mesh=mesh, in_specs=in_specs, out_specs=out_specs, check_vma=False
    )
```

time: 185 us -> 26.4 us (0.14); the launches traced: 182 us -> 26.1 us
  blocking collectives: 90.4 us -> 0 us
  starting transfers between devices: 24.1 us -> 0 us
  matrix products: 22.4 us -> 0 us
  Pallas kernels: 0 us -> 20 us
  other arithmetic: 14.4 us -> 0 us
  local copies, waits for them, and re-layouts: 14.4 us -> 3.67 us
  loops' own time: 8.5 us -> 0 us
  waiting for transfers between devices: 2.99 us -> 0 us
  between operations: 4.84 us -> 2.46 us
    psum x1 -> x0, blocking collectives: 90.4 us -> none  [on_device(): totals = lax.psum((squared, counted), ('blk', 'help'))]
    ppermute x4 -> x0, starting transfers between devices: 24.1 us -> none  [passed_along(): return lax.ppermute(block, axis, route)]
    dot_general x30 -> x0, matrix products: 22.4 us -> none  [the longest x6 6.48 us: one_block(): jnp.einsum('tk,tbr->kbr', item_onehot, item_terms, precision=lax.Precisio...]
    pallas_call x0 -> x1, Pallas kernels: none -> 20 us  [on_device(): pl.pallas_call(functools.partial(kernel, sizes), out_shape=(jax.ShapeDtyp...]
    another operation x4 -> x0, loops' own time: 8.5 us -> none  [tile_terms(): return lax.fori_loop(0, blocks, one_block, start_carry)]
    gather x12 -> x0, local copies, waits for them, and re-layouts: 6.87 us -> none  [the longest x6 3.43 us: one_block(): user_part = jnp.take(user_grid, user_ids, axis=0)]
    reduce_sum x14 -> x0, other arithmetic: 5.74 us -> none  [the longest x6 4.53 us: one_block(): jnp.sum(weight)]
    and x12 -> x0, other arithmetic: 5.04 us -> none  [the longest x6 4.49 us: one_block(): item_part = jnp.take(item_grid, item_ids, axis=0)]
  transfers between devices with their start and end apart: 4 -> 0, of which waited for: 1 -> 0; matrix products, arithmetic and copies ran while one was open for 8% -> 0% of each run, Pallas kernels for 0% -> 0%
where the time goes in v1:
time: 26.4 us; the launch traced here: 26.1 us
  Pallas kernels  20 us (76%)
  local copies, waits for them, and re-layouts  3.67 us (14%)
  between operations  2.46 us (9%)
    pallas_call x1, Pallas kernels, on_device(): pl.pallas_call(functools.partial(kernel, sizes), out_shape=(jax.ShapeDtyp...  20 us
    unnamed x10, local copies, waits for them, and re-layouts  3.67 us

profile of v1, /device:TPU:0, one launch (start us, length us, event | category | flops | bytes accessed | tf_op | source)
XLA Modules:
  0.0 26.1 jit_solution(3695945937297792884)
XLA Ops:
  0.6 20.0 %block_steps.1 = (f32[512,128]{1,0:T(8,128)}, f32[512,128]{1,0:T(8,128)}, f32[4,128]{1,0:T(4,128)}, f32[1,512]{1,0:T(1,128)}, f32[1]{0:T(128)}) custom-call(s32[1,1,2,16]{3,2,1,0:T(2,128)} %cells_ref.1, f32[512,128]{1,0:T(8,128)} %users_ref.1, f32[512,128]{1,0:T(8,128)} %items_ref.1, f32[4,128]{1,0:T(4,128)} %bitcast.4, f32[1,512]{1,0:T(1,128)} %bitcast.5, ...), custom_call_target="tpu_custom_call" | custom-call | tf_op jit(solution)/shard_map/block_steps/pallas_call | solution.py:237
  20.6 0.0 copy-start
  20.6 1.7 %copy.17 = f32[512,128]{1,0:T(8,128)} copy(f32[512,128]{1,0:T(8,128)} %get-tuple-element.20) | data formatting | bytes 524288
  22.4 0.0 copy-done
  22.4 0.0 copy-start.2
  22.4 0.7 %copy.18 = f32[512,128]{1,0:T(8,128)} copy(f32[512,128]{1,0:T(8,128)S(1)} %copy-done) | data formatting | bytes 524288
  23.1 0.0 copy-done.2
  23.1 0.0 copy-start.1
  23.1 0.6 %copy.19 = f32[512]{0:T(512)} copy(f32[512]{0:T(512)S(1)} %bitcast.7) | data formatting | bytes 4096
  23.6 0.1 copy-done.1
  23.7 0.6 %copy.20 = f32[512]{0:T(512)} copy(f32[512]{0:T(512)S(1)} %bitcast.6) | data formatting | bytes 4096
Async XLA Ops:
  20.6 1.7 %copy-start = (f32[512,128]{1,0:T(8,128)S(1)}, f32[512,128]{1,0:T(8,128)}, u32[]{:S(2)}) copy-start(f32[512,128]{1,0:T(8,128)} %get-tuple-element.21) | copy-start | bytes 786436
  22.4 0.7 %copy-start.2 = (f32[4,128]{1,0:T(4,128)S(1)}, f32[4,128]{1,0:T(4,128)}, u32[]{:S(2)}) copy-start(f32[4,128]{1,0:T(4,128)} %get-tuple-element.12) | copy-start | bytes 6148
  23.1 0.7 %copy-start.1 = (f32[1,512]{1,0:T(1,128)S(1)}, f32[1,512]{1,0:T(1,128)}, u32[]{:S(2)}) copy-start(f32[1,512]{1,0:T(1,128)} %get-tuple-element.13) | copy-start | bytes 6148

commit v2 on v1

--- a/solution.py
+++ b/solution.py
@@ -13,6 +13,7 @@
 DECAY = 0.02
 LEVELS = 32767.0
 CHUNK = 256
+VMEM = 56 * 1024 * 1024
 MESH = pl.DeviceIdType.MESH
 F32 = jnp.float32
 BF16 = jnp.bfloat16
@@ -39,10 +40,10 @@
 def kernel(
     sizes,
     cells_ref, users_ref, items_ref, ustate_ref, istate_ref, ratings_ref, masks_ref,
-    users_out, items_out, ustate_out, istate_out, loss_ref,
-    users, items_nat, items, ustate_in, ustate_row, ustate, istate, error,
+    users, items_nat, ustate_row, istate, loss_ref,
+    items, ustate_in, ustate, error,
     items_back, codes_out, aux_out, codes_in, aux_in, sums_help, sums_blk,
-    load_sem, store_sem, code_send, code_recv, aux_send, aux_recv,
+    load_sem, code_send, code_recv, aux_send, aux_recv,
     help_send, help_recv, blk_send, blk_recv, *tiles,
 ):
     strata, capacity, tile, rank, user_tiles, item_tiles, n_blk, n_help = sizes
@@ -165,12 +166,8 @@
                 ustate[rows, :] = state
                 users[rows, :] = own - (LEARN * grad) * lax.rsqrt(state + EPS)
 
-    stores = [pltpu.make_async_copy(users, users_out, store_sem.at[0])]
-    stores[-1].start()
     for u in range(user_tiles):
         ustate_row[u:u + 1, :] = ustate[u * tile:(u + 1) * tile, :].T[0:1, :]
-    stores.append(pltpu.make_async_copy(ustate_row, ustate_out, store_sem.at[1]))
-    stores[-1].start()
 
     def arrival(buf, axis, index, send, recv):
         return pltpu.make_async_remote_copy(
@@ -200,18 +197,14 @@
         istate[0:1, lo:lo + CHUNK] = aux_in[strata - 1, c, 1:2, :]
         for k in range(per_chunk):
             items_nat[lo + k * tile:lo + (k + 1) * tile, :] = block[:, k * tile:(k + 1) * tile].T
-        rows = pl.ds(lo, CHUNK)
-        stores.append(pltpu.make_async_copy(items_nat.at[rows], items_out.at[rows], store_sem.at[3 + c]))
-        stores[-1].start()
-    stores.append(pltpu.make_async_copy(istate, istate_out, store_sem.at[2]))
-    stores[-1].start()
 
     for d in range(1, n_blk):
         arrival(sums_blk, "blk", lax.rem(my_blk + d, n_blk), blk_send, blk_recv).wait_recv()
     total = sums_blk[0]
     for j in range(1, n_blk):
         total = total + sums_blk[j]
-    loss_ref[0] = jnp.sum(total[0:1, :]) / jnp.sum(total[1:2, :])
+    loss_ref[...] = jnp.broadcast_to(
+        jnp.sum(total[0:1, :], axis=1, keepdims=True) / jnp.sum(total[1:2, :], axis=1, keepdims=True), (1, tile))
 
     for copy in helps + blks:
         copy.wait_send()
@@ -219,7 +212,15 @@
         for c in range(chunks):
             for copy in shift(hop, c):
                 copy.wait_send()
-    for copy in stores:
+
+
+def deliver(users, items, ustate, istate, loss, users_out, items_out, ustate_out, istate_out, loss_out, scalar, sems):
+    scalar[0] = loss[0, 0]
+    pairs = ((users, users_out), (items, items_out), (ustate, ustate_out), (istate, istate_out), (scalar, loss_out))
+    copies = [pltpu.make_async_copy(src, dst, sems.at[n]) for n, (src, dst) in enumerate(pairs)]
+    for copy in copies:
+        copy.start()
+    for copy in copies:
         copy.wait()
 
 
@@ -233,26 +234,23 @@
     sizes = (strata, capacity, tile, rank, user_tiles, item_tiles, n_blk, n_help)
     hbm = pl.BlockSpec(memory_space=pl.ANY)
     smem = pl.BlockSpec(memory_space=pltpu.SMEM)
+    vmem = pl.BlockSpec(memory_space=pltpu.VMEM)
     dma = pltpu.SemaphoreType.DMA
     outs = pl.pallas_call(
         functools.partial(kernel, sizes),
         out_shape=(
-            jax.ShapeDtypeStruct(users.shape, F32),
-            jax.ShapeDtypeStruct(items.shape, F32),
-            jax.ShapeDtypeStruct((user_tiles, tile), F32),
-            jax.ShapeDtypeStruct((1, n_items), F32),
-            jax.ShapeDtypeStruct((1,), F32),
+            pltpu.VMEM(users.shape, F32),
+            pltpu.VMEM(items.shape, F32),
+            pltpu.VMEM((user_tiles, tile), F32),
+            pltpu.VMEM((1, n_items), F32),
+            pltpu.VMEM((1, tile), F32),
         ),
         in_specs=[smem] + [hbm] * 6,
-        out_specs=(hbm, hbm, hbm, hbm, smem),
+        out_specs=(vmem,) * 5,
         scratch_shapes=[
-            pltpu.VMEM((n_users, rank), F32),
-            pltpu.VMEM((n_items, rank), F32),
             pltpu.VMEM((rank, n_items), F32),
             pltpu.VMEM((user_tiles, tile), F32),
-            pltpu.VMEM((user_tiles, tile), F32),
             pltpu.VMEM((n_users, tile), F32),
-            pltpu.VMEM((1, n_items), F32),
             pltpu.VMEM((n_users, n_items), BF16),
             pltpu.VMEM((n_items, rank), BF16),
             pltpu.VMEM((strata, chunks, rank, CHUNK), jnp.int16),
@@ -262,17 +260,25 @@
             pltpu.VMEM((n_help, 8, tile), F32),
             pltpu.VMEM((n_blk, 8, tile), F32),
             dma((4 + 2 * strata,)),
-            dma((3 + chunks,)),
             dma((strata, chunks)), dma((strata, chunks)),
             dma((strata, chunks)), dma((strata, chunks)),
             dma((n_help,)), dma((n_help,)),
             dma((n_blk,)), dma((n_blk,)),
         ] + [pltpu.VMEM((capacity, tile, tile), BF16)] * (2 * strata),
         compiler_params=pltpu.CompilerParams(
-            collective_id=0, has_side_effects=True, vmem_limit_bytes=56 * 1024 * 1024
+            collective_id=0, has_side_effects=True, vmem_limit_bytes=VMEM
         ),
         name="block_steps",
     )(tile_cells, users, items, user_state.reshape(user_tiles, tile), item_state.reshape(1, n_items), ratings, masks)
+    outs = pl.pallas_call(
+        deliver,
+        out_shape=[jax.ShapeDtypeStruct(out.shape, F32) for out in outs[:4]] + [jax.ShapeDtypeStruct((1,), F32)],
+        in_specs=[vmem] * 5,
+        out_specs=[hbm] * 5,
+        scratch_shapes=[pltpu.SMEM((1,), F32), dma((5,))],
+        compiler_params=pltpu.CompilerParams(vmem_limit_bytes=4 * 1024 * 1024),
+        name="deliver",
+    )(*outs)
     users_out, items_out, ustate_out, istate_out, loss = outs
     return users_out, items_out, ustate_out.reshape(n_users), istate_out.reshape(n_items), loss
 

time: 26.4 us -> 21 us (0.80)
  local copies, waits for them, and re-layouts: 3.67 us -> 0 us
  between operations: 2.46 us -> 0.64 us
    unnamed x10 -> x0, local copies, waits for them, and re-layouts: 3.67 us -> none
    pallas_call x1 -> x2, Pallas kernels: 20 us -> 20.2 us  [the longest x1 19.4 us: on_device(): pl.pallas_call(functools.partial(kernel, sizes), out_shape=(pltpu.VMEM(us...]
where the time goes in v2:
time: 21 us; the launch traced here: 20.9 us
  Pallas kernels  20.2 us (96%)
  between operations  0.64 us (3%)
    pallas_call x1, Pallas kernels, on_device(): pl.pallas_call(functools.partial(kernel, sizes), out_shape=(pltpu.VMEM(us...  19.4 us
    pallas_call x1, Pallas kernels, on_device(): pl.pallas_call(deliver, out_shape=[jax.ShapeDtypeStruct(out.shape, F32) f...  0.85 us

profile of v2, /device:TPU:0, one launch (start us, length us, event | category | flops | bytes accessed | tf_op | source)
XLA Modules:
  0.0 20.9 jit_solution(8150242548604509150)
XLA Ops:
  0.6 19.4 %block_steps.1 = (f32[512,128]{1,0:T(8,128)S(1)}, f32[512,128]{1,0:T(8,128)S(1)}, f32[4,128]{1,0:T(4,128)S(1)}, f32[1,512]{1,0:T(1,128)S(1)}, f32[1,128]{1,0:T(1,128)S(1)}) custom-call(s32[1,1,2,16]{3,2,1,0:T(2,128)} %cells_ref.1, f32[512,128]{1,0:T(8,128)} %users_ref.1, f32[512,128]{1,0:T(8,128)} %items_ref.1, f32[4,128]{1,0:T(4,128)} %bitcast.4, ...), custom_call_target="tpu_custom_call" | custom-call | tf_op jit(solution)/shard_map/block_steps/pallas_call | solution.py:239
  20.0 0.8 %deliver.1 = (f32[512,128]{1,0:T(8,128)}, f32[512,128]{1,0:T(8,128)}, f32[4,128]{1,0:T(4,128)}, f32[1,512]{1,0:T(1,128)}, f32[1]{0:T(128)}) custom-call(f32[512,128]{1,0:T(8,128)S(1)} %get-tuple-element.15.users, f32[512,128]{1,0:T(8,128)S(1)} %get-tuple-element.16.items, f32[4,128]{1,0:T(4,128)S(1)} %get-tuple-element.17.ustate, ...), custom_call_target="tpu_custom_call" | custom-call | tf_op jit(solution)/shard_map/deliver/pallas_call | solution.py:273

commit v3 on v2

--- a/solution.py
+++ b/solution.py
@@ -71,7 +71,7 @@
     for d in range(1, n_help):
         pl.semaphore_signal(barrier, inc=1, device_id={"help": lax.rem(my_help + d, n_help)}, device_id_type=MESH)
 
-    slots = [inverse_cells(cells_ref, s, capacity) for s in range(strata)]
+    slots = [inverse_cells(cells_ref, 0, capacity)]
 
     loads["items"].wait()
     for i in range(item_tiles):
@@ -101,6 +101,8 @@
         return x.reshape(-1, 8, tile).sum(axis=0)
 
     for s in range(strata):
+        if s > 0:
+            slots.append(inverse_cells(cells_ref, s, capacity))
         loads[("m", s)].wait()
         loads[("r", s)].wait()
         for inner in range(INNER):
@@ -131,6 +133,19 @@
                         if inner == 0:
                             counted = counted + fold(weight)
                         error[u * tile:(u + 1) * tile, i * tile:(i + 1) * tile] = err.astype(BF16)
+                if s == strata - 1 and last and c == chunks - 1:
+                    mine = jnp.concatenate(
+                        [jnp.sum(squared, axis=0, keepdims=True),
+                         jnp.sum(counted, axis=0, keepdims=True) * float(INNER),
+                         jnp.zeros((6, tile), F32)], axis=0)
+                    sums_help[my_help] = mine
+                    helps = []
+                    for d in range(1, n_help):
+                        helps.append(pltpu.make_async_remote_copy(
+                            src_ref=sums_help.at[my_help], dst_ref=sums_help.at[my_help],
+                            send_sem=help_send.at[d], recv_sem=help_recv.at[my_help],
+                            device_id={"help": lax.rem(my_help + d, n_help)}, device_id_type=MESH))
+                        helps[-1].start()
                 grad = jnp.dot(ut, error[:, lo:hi], preferred_element_type=F32) + DECAY * block
                 state = istate[0:1, lo:hi] + jnp.sum(grad * grad, axis=0, keepdims=True) * (1.0 / rank)
                 block = block - (LEARN * grad) * lax.rsqrt(state + EPS)
@@ -145,19 +160,6 @@
                         pl.semaphore_wait(barrier, (n_blk - 1) + (n_help - 1))
                     for copy in shift(s, c):
                         copy.start()
-            if s == strata - 1 and last:
-                mine = jnp.concatenate(
-                    [jnp.sum(squared, axis=0, keepdims=True),
-                     jnp.sum(counted, axis=0, keepdims=True) * float(INNER),
-                     jnp.zeros((6, tile), F32)], axis=0)
-                sums_help[my_help] = mine
-                helps = []
-                for d in range(1, n_help):
-                    helps.append(pltpu.make_async_remote_copy(
-                        src_ref=sums_help.at[my_help], dst_ref=sums_help.at[my_help],
-                        send_sem=help_send.at[d], recv_sem=help_recv.at[my_help],
-                        device_id={"help": lax.rem(my_help + d, n_help)}, device_id_type=MESH))
-                    helps[-1].start()
             for u in range(user_tiles):
                 rows = slice(u * tile, (u + 1) * tile)
                 own = users[rows, :]

time: 21 us -> 20.8 us (level)
    pallas_call x1, Pallas kernels: 19.4 us -> 19.2 us  [on_device(): pl.pallas_call(functools.partial(kernel, sizes), out_shape=(pltpu.VMEM(us...]
where the time goes in v3:
time: 20.8 us; the launch traced here: 20.7 us
  Pallas kernels  20 us (96%)
  between operations  0.64 us (3%)
    pallas_call x1, Pallas kernels, on_device(): pl.pallas_call(functools.partial(kernel, sizes), out_shape=(pltpu.VMEM(us...  19.2 us
    pallas_call x1, Pallas kernels, on_device(): pl.pallas_call(deliver, out_shape=[jax.ShapeDtypeStruct(out.shape, F32) f...  0.85 us

profile of v3, /device:TPU:0, one launch (start us, length us, event | category | flops | bytes accessed | tf_op | source)
XLA Modules:
  0.0 20.7 jit_solution(16735630893111267603)
XLA Ops:
  0.6 19.2 %block_steps.1 = (f32[512,128]{1,0:T(8,128)S(1)}, f32[512,128]{1,0:T(8,128)S(1)}, f32[4,128]{1,0:T(4,128)S(1)}, f32[1,512]{1,0:T(1,128)S(1)}, f32[1,128]{1,0:T(1,128)S(1)}) custom-call(s32[1,1,2,16]{3,2,1,0:T(2,128)} %cells_ref.1, f32[512,128]{1,0:T(8,128)} %users_ref.1, f32[512,128]{1,0:T(8,128)} %items_ref.1, f32[4,128]{1,0:T(4,128)} %bitcast.4, ...), custom_call_target="tpu_custom_call" | custom-call | tf_op jit(solution)/shard_map/block_steps/pallas_call | solution.py:241
  19.8 0.8 %deliver.1 = (f32[512,128]{1,0:T(8,128)}, f32[512,128]{1,0:T(8,128)}, f32[4,128]{1,0:T(4,128)}, f32[1,512]{1,0:T(1,128)}, f32[1]{0:T(128)}) custom-call(f32[512,128]{1,0:T(8,128)S(1)} %get-tuple-element.15.users, f32[512,128]{1,0:T(8,128)S(1)} %get-tuple-element.16.items, f32[4,128]{1,0:T(4,128)S(1)} %get-tuple-element.17.ustate, ...), custom_call_target="tpu_custom_call" | custom-call | tf_op jit(solution)/shard_map/deliver/pallas_call | solution.py:275
